TPU v7x, 32 devices: a whole 2x2x4 slice. The times are simulated.
32 devices in a mesh: heads: 4 (over y, x), ctx: 8 (over z, core).
Axes of the slice: x: 2, y: 2, z: 4, core: 2. Of those that a mesh axis runs over, the one named last changes fastest.
Arguments:
- query_vectors: bfloat16 [1024, 4, 640], P('ctx', 'heads'), may hold values from -6 to 6
- key_vectors: bfloat16 [1024, 4, 128], P('ctx', 'heads'), may hold values from -6 to 6
- value_vectors: bfloat16 [1024, 4, 128], P('ctx', 'heads'), may hold values from -6 to 6
- log_gate: float32 [4, 1024], P('heads', 'ctx'), may hold values from -1 to 0, as said below
- doc_start: int32 [8], P('ctx'), may hold values from 1 to 128
- norm_gain: float32 [4, 640], P('heads'), may hold values from 0.1 to 1.9
- out_weight: bfloat16 [2560, 5120], P('heads'), may hold values from -0.125 to 0.125
Outputs:
- mixed_out: bfloat16 [1024, 5120], P('ctx', 'heads')
- prefix_state: bfloat16 [4, 8, 8256, 128], P('heads', 'ctx')
Inputs may be any that keep to these rules, and one draw needn't show every extreme that they name: log_gate is never positive.
All inputs are finite; a program needn't handle non-finite values.
Results may differ from a plain program's by a relative error of at most 0.014.
Values may be sent and summed in bfloat16 or wider, within the bound.
A program may use at most 192 MiB of HBM per device.

v0:
```python
import functools
import math

import jax
import jax.numpy as jnp
from jax import lax
from jax.experimental import pallas as pl
from jax.experimental.pallas import tpu as pltpu
from jax.sharding import PartitionSpec as P

ROOT_TWO = math.sqrt(2.0)
NT = (((1,), (1,)), ((), ()))
PER_STEP = 8
CHUNK = 8


def offset(i, size):
    return i * size - i * (i - 1) // 2


def attend_kernel(block, groups, q_ref, own_ref, all_ref, wt_ref, cum_ref, doc_ref, gain_ref, out_ref):
    size = q_ref.shape[1] // groups
    slots = all_ref.shape[0]
    f32 = jnp.float32
    queries = jnp.concatenate([q_ref[:, g * size : (g + 1) * size] for g in range(groups)], axis=0)
    boundary = doc_ref[0]
    cum_row = jnp.broadcast_to(cum_ref[...], (block, block))
    cum_col = cum_row.T
    at_t = lax.broadcasted_iota(jnp.int32, (block, block), 0)
    at_s = lax.broadcasted_iota(jnp.int32, (block, block), 1)
    allowed = (at_s <= at_t) & jnp.logical_not((at_s < boundary) & (at_t >= boundary))
    decay = jnp.where(allowed, jnp.exp(jnp.minimum(cum_col - cum_row, 0.0)), 0.0)
    read = jnp.where(at_t < boundary, jnp.exp(cum_col), 0.0)

    def part(keys, values, factor):
        products = lax.dot_general(queries, keys, NT, preferred_element_type=f32)
        scores = products * products * jnp.concatenate([factor] * groups, axis=0)
        return jnp.dot(scores.astype(jnp.bfloat16), values, preferred_element_type=f32)

    summed = part(own_ref[:, :size], own_ref[:, size:], decay)
    per = min(CHUNK, slots)
    for first in range(0, slots, per):
        keys = all_ref[first : first + per, :block, :size].reshape(per * block, size)
        values = all_ref[first : first + per, :block, size:].reshape(per * block, size)
        factor = jnp.concatenate(
            [read * wt_ref[:, (first + c) * block : (first + c + 1) * block] for c in range(per)], axis=1
        )
        summed = summed + part(keys, values, factor)
    normed = summed * lax.rsqrt(jnp.mean(summed * summed, axis=-1, keepdims=True) + 1e-6)
    for g in range(groups):
        lanes = slice(g * size, (g + 1) * size)
        rows = normed[g * block : (g + 1) * block]
        out_ref[:, lanes] = (rows * gain_ref[:, lanes]).astype(out_ref.dtype)


def state_kernel(block, all_ref, wt_ref, out_ref, keys_t, scaled, values, acc):
    slots = all_ref.shape[0]
    size = all_ref.shape[2] // 2
    per = min(CHUNK, slots)
    chunks = slots // per
    span = per * block

    def chunk(index):
        for c in range(per):
            lanes = slice(c * block, (c + 1) * block)
            turned = all_ref[index * per + c, :block, :size].astype(jnp.float32).T
            keys_t[:, lanes] = turned.astype(jnp.bfloat16)
            weight = wt_ref[:, pl.ds(pl.multiple_of((index * per + c) * block, block), block)]
            scaled[:, lanes] = turned * weight
            values[lanes, :] = all_ref[index * per + c, :block, size:]
        for a in range(size - 16, -1, -16):
            rows = size - a

            def step(s, carry):
                pieces = []
                firsts = []
                for u in range(PER_STEP):
                    i = a + 15 - (s * PER_STEP + u)
                    row = jnp.broadcast_to(scaled[pl.ds(i, 1), :], (16, span)).astype(jnp.bfloat16)
                    pieces.append(
                        (keys_t[a:, :].reshape(rows // 16, 16, span) * row[None]).reshape(rows, span)
                    )
                    firsts.append(i)
                product = jnp.dot(
                    jnp.concatenate(pieces, axis=0), values[...], preferred_element_type=jnp.float32
                )
                at = lax.broadcasted_iota(jnp.int32, (rows, size), 0) + a
                for u, i in enumerate(firsts):
                    piece = product[u * rows : (u + 1) * rows]
                    piece = jnp.where(at == i, piece, piece * ROOT_TWO)
                    place = pl.ds(offset(i, size) - (i - a), rows)
                    if chunks == 1:
                        acc[place, :] = piece
                    else:
                        acc[place, :] = acc[place, :] + jnp.where(at < i, 0.0, piece)
                return carry

            lax.fori_loop(0, 16 // PER_STEP, step, 0)

    if chunks == 1:
        chunk(0)
    else:
        acc[...] = jnp.zeros_like(acc)
        lax.fori_loop(0, chunks, lambda index, carry: (chunk(index), carry)[1], 0)
    out_ref[...] = acc[...].astype(out_ref.dtype)


def token_weights(gates, starts, me):
    slots, block = gates.shape
    token = jnp.arange(block, dtype=jnp.int32)
    cumulative = jnp.sum(
        jnp.where(token[None, :, None] >= token[None, None, :], gates[:, None, :], 0.0), axis=2
    )
    total = cumulative[:, -1]
    slot = jnp.arange(slots, dtype=jnp.int32)
    between = (slot[None, :] > slot[:, None]) & (slot[None, :] < me)
    later = jnp.sum(jnp.where(between, total[None, :], 0.0), axis=1)
    cut = jnp.any(between & (starts < block)[None, :], axis=1)
    begin = jnp.where(starts < block, starts, 0)
    live = (slot < me) & jnp.logical_not(cut)
    keep = live[:, None] & (token[None, :] >= begin[:, None])
    exponent = (total[:, None] - cumulative) + later[:, None]
    return jnp.where(keep, jnp.exp(exponent), 0.0)


def on_device(query_vectors, key_vectors, value_vectors, log_gate, doc_start, norm_gain, out_weight):
    bf16, f32 = jnp.bfloat16, jnp.float32
    block, _, size = key_vectors.shape
    groups = query_vectors.shape[2] // size
    features = size * (size + 1) // 2
    me = lax.axis_index("ctx")
    slots = lax.axis_size("ctx")

    gate = log_gate
    high = lax.reduce_precision(gate, 8, 7)
    middle = lax.reduce_precision(gate - high, 8, 7)
    low = gate - high - middle
    start = jnp.broadcast_to(doc_start.astype(f32)[:, None], (1, block))
    extra = jnp.concatenate(
        [jnp.concatenate([high, middle], axis=1), jnp.concatenate([low, start], axis=1)], axis=0
    ).astype(bf16)
    own = jnp.concatenate([key_vectors[:, 0, :], value_vectors[:, 0, :]], axis=1)
    sent = jnp.concatenate([own, jnp.pad(extra, ((0, 14), (0, 0)))], axis=0)
    gathered = lax.all_gather(sent, "ctx", axis=0, tiled=False)

    extras = gathered[:, block : block + 2, :].astype(f32)
    gates = extras[:, 0, :block] + extras[:, 0, block:] + extras[:, 1, :block]
    starts = extras[:, 1, block].astype(jnp.int32)
    weights = token_weights(gates, starts, me).reshape(1, slots * block)
    token = jnp.arange(block, dtype=jnp.int32)
    cumulative = jnp.sum(jnp.where(token[:, None] >= token[None, :], gate, 0.0), axis=1)[None]

    vmem = pl.BlockSpec(memory_space=pltpu.VMEM)
    retained = pl.pallas_call(
        functools.partial(attend_kernel, block, groups),
        out_shape=jax.ShapeDtypeStruct((block, groups * size), bf16),
        in_specs=[vmem] * 5 + [pl.BlockSpec(memory_space=pltpu.SMEM), vmem],
        out_specs=vmem,
        compiler_params=pltpu.CompilerParams(vmem_limit_bytes=48 * 2**20),
    )(query_vectors[:, 0, :], own, gathered, weights, cumulative, doc_start, norm_gain)
    partial = jnp.dot(retained, out_weight, preferred_element_type=f32).astype(bf16)
    mixed_out = lax.psum_scatter(partial, "heads", scatter_dimension=1, tiled=True)

    span = min(CHUNK, slots) * block
    prefix = pl.pallas_call(
        functools.partial(state_kernel, block),
        out_shape=jax.ShapeDtypeStruct((features, size), bf16),
        in_specs=[vmem] * 2,
        out_specs=vmem,
        scratch_shapes=[
            pltpu.VMEM((size, span), bf16),
            pltpu.VMEM((size, span), f32),
            pltpu.VMEM((span, size), bf16),
            pltpu.VMEM((features, size), f32),
        ],
        compiler_params=pltpu.CompilerParams(vmem_limit_bytes=48 * 2**20),
        cost_estimate=pl.CostEstimate(
            flops=2 * features * slots * block * size,
            bytes_accessed=2 * features * size + 4 * slots * block * size,
            transcendentals=0,
        ),
    )(gathered, weights)
    return (mixed_out, prefix[None, None])


def solution(mesh):
    placed = (
        P("ctx", "heads", None),
        P("ctx", "heads", None),
        P("ctx", "heads", None),
        P("heads", "ctx"),
        P("ctx"),
        P("heads", None),
        P("heads", None),
    )
    return jax.shard_map(
        on_device,
        mesh=mesh,
        in_specs=placed,
        out_specs=(P("ctx", "heads"), P("heads", "ctx", None, None)),
        check_vma=False,
    )
```

profile of v0, /device:TPU:0, one launch (start us, length us, event | category | flops | bytes accessed | tf_op | source)
XLA Modules:
  0.0 74.1 jit_solution(1157234760392974385)
XLA Ops:
  7.2 0.0 reduce-scatter.2.cloned.1.call-start
  7.9 0.7 reduce-precision_convert_fusion.1
  8.6 0.8 %pad_maximum_fusion.own_ref = bf16[128,256]{1,0:T(8,128)(2,1)S(1)} fusion(bf16[128,128]{1,0:T(8,128)(2,1)} %bitcast.19, bf16[128,128]{1,0:T(8,128)(2,1)} %bitcast.21), kind=kLoop, calls=%fused_computation.5 | loop fusion | flops 131072 | bytes 131072 | tf_op jit(solution)/shard_map/concatenate | solution.py:142
  9.3 0.8 %fusion.1 = bf16[144,256]{1,0:T(8,128)(2,1)S(1)} fusion(bf16[2,256]{1,0:T(2,128)(2,1)S(1)} %fusion.7, bf16[128,128]{1,0:T(8,128)(2,1)} %bitcast.20, bf16[128,128]{1,0:T(8,128)(2,1)} %bitcast.22), kind=kLoop, calls=%fused_computation.4 | loop fusion | flops 294912 | bytes 140288 | tf_op jit(solution)/shard_map/concatenate | solution.py:143
  10.1 16.6 %all-gather = bf16[1152,256]{1,0:T(8,128)(2,1)S(1)} all-gather(bf16[144,256]{1,0:T(8,128)(2,1)S(1)} %fusion.1), channel_id=2, replica_groups=mesh['heads'=4,'ctx'=8] {'ctx'}, dimensions={0}, use_global_device_ids=true | all-gather | bytes 663552 | tf_op jit(solution)/shard_map/all_gather | solution.py:144
  26.8 0.2 fusion.2
  27.0 0.8 %select_reduce_fusion.1 = f32[128]{0:T(128)S(1)} fusion(f32[128]{0:T(128)} %bitcast.24), kind=kLoop, calls=%fused_computation.6 | loop fusion | flops 49024 | bytes 1024 | tf_op jit(solution)/shard_map/reduce_sum | solution.py:151
  27.8 0.2 select_reduce_fusion
  28.0 0.2 slice_reduce_fusion
  28.2 0.1 fusion.5
  28.3 0.1 select_reduce_fusion.2
  28.5 0.1 exponential_select_fusion
  28.5 0.0 copy-start
  28.5 0.9 %copy-done = bf16[128,1,640]{2,0,1:T(8,128)(2,1)S(1)} copy-done((bf16[128,1,640]{2,0,1:T(8,128)(2,1)S(1)}, bf16[128,1,640]{2,0,1:T(8,128)(2,1)}, u32[]{:S(2)}) %copy-start) | copy-done | bytes 163864
  29.5 0.0 copy-start.1
  29.5 0.7 copy-done.1
  30.1 1.1 %shard_map.86 = bf16[128,640]{1,0:T(8,128)(2,1)S(1)} custom-call(bf16[128,640]{1,0:T(8,128)(2,1)S(1)} %bitcast.15, bf16[128,256]{1,0:T(8,128)(2,1)S(1)} %pad_maximum_fusion.own_ref, bf16[8,144,256]{2,1,0:T(8,128)(2,1)S(1)} %bitcast.13, f32[1,1024]{1,0:T(1,128)S(1)} %bitcast.16, f32[1,128]{1,0:T(1,128)S(1)} %bitcast.18, s32[1]{0:T(128)S(6)} %copy.11.doc_ref, ...), custom_call_target="tpu_custom_call" | custom-call | tf_op jit(solution)/shard_map/pallas_call | solution.py:154
  31.3 5.2 %convolution_convert_fusion = bf16[128,5120]{1,0:T(8,128)(2,1)} fusion(bf16[128,640]{1,0:T(8,128)(2,1)S(1)} %shard_map.86, bf16[640,5120]{1,0:T(8,128)(2,1)} %param.13), kind=kOutput, calls=%fused_computation | convolution fusion | flops 839516160 | bytes 8028160 | tf_op jit(solution)/shard_map/dot_general | solution.py:161
  36.5 0.0 reduce-scatter.2.cloned.1.call-update
  36.5 9.2 %shard_map.87 = bf16[8256,128]{1,0:T(8,128)(2,1)} custom-call(bf16[8,144,256]{2,1,0:T(8,128)(2,1)S(1)} %bitcast.14, f32[1,1024]{1,0:T(1,128)S(1)} %bitcast.17), custom_call_target="tpu_custom_call" | custom-call | flops 2164260864 | bytes 2637824 | tf_op jit(solution)/shard_map/pallas_call | solution.py:165
  45.7 21.5 %reduce-scatter.2.cloned.1.call-done = bf16[128,1280]{1,0:T(8,128)(2,1)} async-done(((bf16[128,5120]{1,0:T(8,128)(2,1)}), bf16[128,1280]{1,0:T(8,128)(2,1)}) %reduce-scatter.2.cloned.1.call-update) | async-done | bytes 327696 | tf_op jit(solution)/shard_map/reduce_scatter | solution.py:162
  (7 shorter events, 0.1 us)
Async XLA Ops:
  7.2 60.1 %reduce-scatter.2.cloned.1.call-start = ((), (), s32[]{:S(2)}) async-start(), calls=%async_computation.1 | async-start | bytes 1638400 | tf_op jit(solution)/shard_map/reduce_scatter | solution.py:162
  28.5 0.9 %copy-start = (bf16[128,1,640]{2,0,1:T(8,128)(2,1)S(1)}, bf16[128,1,640]{2,0,1:T(8,128)(2,1)}, u32[]{:S(2)}) copy-start(bf16[128,1,640]{2,0,1:T(8,128)(2,1)} %param.7) | copy-start | bytes 491524
  29.5 0.7 copy-start.1
Sparse Core Ops, SparseCore 0:
  36.6 30.5 reduce-scatter.1
where the time goes:
time: 74.4 us; the launch traced here: 74.1 us
  waiting for transfers between devices  21.5 us (29%)
  blocking collectives  16.6 us (22%)
  between operations  14.7 us (20%)
  Pallas kernels  10.4 us (14%)
  matrix products  5.19 us (7%)
  other arithmetic  3.83 us (5%)
  local copies, waits for them, and re-layouts  1.79 us (2%)
    reduce_scatter x1, waiting for transfers between devices, on_device(): lax.psum_scatter(partial, 'heads', scatter_dimension=1, tiled=True)  21.5 us
    all_gather x1, blocking collectives, on_device(): gathered = lax.all_gather(sent, 'ctx', axis=0, tiled=False)  16.6 us
    pallas_call x1, Pallas kernels, on_device(): pl.pallas_call(functools.partial(state_kernel, block), out_shape=jax.Shap...  9.21 us
    dot_general x1, matrix products, on_device(): jnp.dot(retained, out_weight, preferred_element_type=f32).astype(bf16)  5.19 us
    unnamed x4, local copies, waits for them, and re-layouts  1.61 us
  transfers between devices with their start and end apart: 1, of which 1 were waited for; matrix products, arithmetic and copies ran while one was open for 0% of the time, Pallas kernels for 12%

commit v1 on v0

v1 whole, which is shorter than its diff:
```python
import functools
import math

import jax
import jax.numpy as jnp
from jax import lax
from jax.experimental import pallas as pl
from jax.experimental.pallas import tpu as pltpu
from jax.sharding import PartitionSpec as P

ROOT_TWO = math.sqrt(2.0)
NT = (((1,), (1,)), ((), ()))
MESH = pl.DeviceIdType.MESH
PER_STEP = 8
CHUNK = 8
EXTRA = 16


def offset(i, size):
    return i * size - i * (i - 1) // 2


def running_sum(rows):
    lane = lax.broadcasted_iota(jnp.int32, rows.shape, 1)
    shift = 1
    while shift < rows.shape[1]:
        rows = rows + jnp.where(lane >= shift, pltpu.roll(rows, shift, axis=1), 0.0)
        shift *= 2
    return rows


def kernel(
    slots, heads, q_ref, k_ref, v_ref, gate_ref, doc_ref, gain_ref, weight_hbm,
    mixed_ref, prefix_ref,
    shared, token_weight, projection, retained, outgoing, incoming, keys_t, scaled, values, acc,
    load_sem, gather_send, gather_recv, part_send, part_recv,
):
    bf16, f32 = jnp.bfloat16, jnp.float32
    block, size = k_ref.shape
    groups = q_ref.shape[1] // size
    width = mixed_ref.shape[1]
    me = lax.axis_index("ctx")
    head = lax.axis_index("heads")
    outer, core = me // 2, me % 2
    outers = slots // 2
    twin = outer * 2 + 1 - core

    loads = []
    for c in range(heads):
        loads.append(
            pltpu.make_async_copy(
                weight_hbm.at[:, c * width : (c + 1) * width], projection.at[c], load_sem.at[c]
            )
        )
        loads[-1].start()

    barrier = pltpu.get_barrier_semaphore()
    line = [lax.rem(outer + o, outers) * 2 + core for o in range(1, outers)]
    for peer in [twin] + line:
        pl.semaphore_signal(barrier, inc=1, device_id={"ctx": peer}, device_id_type=MESH)
    for o in range(1, heads):
        pl.semaphore_signal(
            barrier, inc=1, device_id={"heads": lax.rem(head + o, heads)}, device_id_type=MESH
        )

    gate = gate_ref[...]
    high = gate.astype(bf16)
    middle = (gate - high.astype(f32)).astype(bf16)
    low = (gate - high.astype(f32) - middle.astype(f32)).astype(bf16)
    boundary = doc_ref[0]
    start = jnp.full((1, block), boundary, jnp.int32).astype(f32).astype(bf16)
    shared[me, :block, :] = k_ref[...]
    shared[me, block : 2 * block, :] = v_ref[...]
    shared[me, 2 * block :, :] = jnp.concatenate(
        [high.astype(f32), middle.astype(f32), low.astype(f32), start.astype(f32)]
        + [jnp.zeros((EXTRA - 4, block), f32)],
        axis=0,
    ).astype(bf16)

    pl.semaphore_wait(barrier, outers + heads - 1)

    def move(slot, peer, index):
        return pltpu.make_async_remote_copy(
            src_ref=shared.at[slot],
            dst_ref=shared.at[slot],
            send_sem=gather_send.at[index],
            recv_sem=gather_recv.at[slot],
            device_id={"ctx": peer},
            device_id_type=MESH,
        )

    sends = []
    for o, peer in enumerate(line):
        sends.append(move(me, peer, o))
        sends[-1].start()
    sends.append(move(me, twin, outers - 1))
    sends[-1].start()

    queries = jnp.concatenate([q_ref[:, g * size : (g + 1) * size] for g in range(groups)], axis=0)
    own = running_sum(jnp.broadcast_to(gate, (8, block)))[:1]
    cum_row = jnp.broadcast_to(own, (block, block))
    cum_col = cum_row.T
    at_t = lax.broadcasted_iota(jnp.int32, (block, block), 0)
    at_s = lax.broadcasted_iota(jnp.int32, (block, block), 1)
    allowed = (at_s <= at_t) & jnp.logical_not((at_s < boundary) & (at_t >= boundary))
    decay = jnp.where(allowed, jnp.exp(jnp.minimum(cum_col - cum_row, 0.0)), 0.0)
    read = jnp.where(at_t < boundary, jnp.exp(cum_col), 0.0)

    def part(keys, held, factor):
        products = lax.dot_general(queries, keys, NT, preferred_element_type=f32)
        scores = products * products * jnp.concatenate([factor] * groups, axis=0)
        return jnp.dot(scores.astype(bf16), held, preferred_element_type=f32)

    summed = part(k_ref[...], v_ref[...], decay)

    for o in range(1, outers):
        source = lax.rem(outer + outers - o, outers) * 2 + core
        move(source, twin, 0).wait_recv()
        sends.append(move(source, twin, outers - 1 + o))
        sends[-1].start()
    for o in range(outers):
        source = lax.rem(outer + outers - o, outers) * 2 + 1 - core
        move(source, twin, 0).wait_recv()

    tails = [shared[c, 2 * block :, :].astype(f32) for c in range(slots)]
    cumulative = running_sum(
        jnp.concatenate([tail[0:1] + tail[1:2] + tail[2:3] for tail in tails], axis=0)
    )
    token = lax.broadcasted_iota(jnp.int32, (1, block), 1)
    later = jnp.zeros((1, block), f32)
    alive = jnp.ones((1, block), f32)
    for c in range(slots - 1, -1, -1):
        before = (jnp.full((1, block), me, jnp.int32) > c).astype(f32)
        starts = tails[c][3:4].astype(jnp.int32)
        broken = starts < block
        begin = jnp.where(broken, starts, 0)
        row = cumulative[c : c + 1]
        total = jnp.broadcast_to(row[:, block - 1 : block], (1, block))
        weight = jnp.exp(total - row + later) * (alive * before)
        token_weight[:, c * block : (c + 1) * block] = jnp.where(token >= begin, weight, 0.0)
        later = later + total * before
        alive = alive * jnp.where(broken, 1.0 - before, 1.0)

    per = min(CHUNK, slots)
    for first in range(0, slots, per):
        keys = shared[first : first + per, :block, :].reshape(per * block, size)
        held = shared[first : first + per, block : 2 * block, :].reshape(per * block, size)
        factor = jnp.concatenate(
            [read * token_weight[:, (first + c) * block : (first + c + 1) * block] for c in range(per)],
            axis=1,
        )
        summed = summed + part(keys, held, factor)
    normed = summed * lax.rsqrt(jnp.mean(summed * summed, axis=-1, keepdims=True) + 1e-6)
    for g in range(groups):
        lanes = slice(g * size, (g + 1) * size)
        retained[:, lanes] = (normed[g * block : (g + 1) * block] * gain_ref[:, lanes]).astype(bf16)

    for load in loads:
        load.wait()
    parts = []
    for o in list(range(1, heads)) + [0]:
        target = lax.rem(head + o, heads)
        outgoing[o] = jnp.dot(
            retained[...], projection[target], preferred_element_type=f32
        ).astype(bf16)
        if o:
            parts.append(
                pltpu.make_async_remote_copy(
                    src_ref=outgoing.at[o],
                    dst_ref=incoming.at[o - 1],
                    send_sem=part_send.at[o - 1],
                    recv_sem=part_recv.at[o - 1],
                    device_id={"heads": target},
                    device_id_type=MESH,
                )
            )
            parts[-1].start()

    chunks = slots // per
    span = per * block

    def chunk(index):
        for c in range(per):
            lanes = slice(c * block, (c + 1) * block)
            turned = shared[index * per + c, :block, :].astype(f32).T
            keys_t[:, lanes] = turned.astype(bf16)
            weight = token_weight[:, pl.ds(pl.multiple_of((index * per + c) * block, block), block)]
            scaled[:, lanes] = turned * weight
            values[lanes, :] = shared[index * per + c, block : 2 * block, :]
        for a in range(size - 16, -1, -16):
            rows = size - a

            def step(s, carry):
                pieces = []
                firsts = []
                for u in range(PER_STEP):
                    i = a + 15 - (s * PER_STEP + u)
                    row = jnp.broadcast_to(scaled[pl.ds(i, 1), :], (16, span)).astype(jnp.bfloat16)
                    pieces.append(
                        (keys_t[a:, :].reshape(rows // 16, 16, span) * row[None]).reshape(rows, span)
                    )
                    firsts.append(i)
                product = jnp.dot(
                    jnp.concatenate(pieces, axis=0), values[...], preferred_element_type=jnp.float32
                )
                at = lax.broadcasted_iota(jnp.int32, (rows, size), 0) + a
                for u, i in enumerate(firsts):
                    piece = product[u * rows : (u + 1) * rows]
                    piece = jnp.where(at == i, piece, piece * ROOT_TWO)
                    place = pl.ds(offset(i, size) - (i - a), rows)
                    if chunks == 1:
                        acc[place, :] = piece
                    else:
                        acc[place, :] = acc[place, :] + jnp.where(at < i, 0.0, piece)
                return carry

            lax.fori_loop(0, 16 // PER_STEP, step, 0)

    if chunks == 1:
        chunk(0)
    else:
        acc[...] = jnp.zeros_like(acc)
        lax.fori_loop(0, chunks, lambda index, carry: (chunk(index), carry)[1], 0)
    prefix_ref[...] = acc[...].astype(bf16)

    for send in sends:
        send.wait_send()
    for send in parts:
        send.wait()
    total = outgoing[0].astype(f32)
    for o in range(1, heads):
        total = total + incoming[o - 1].astype(f32)
    mixed_ref[...] = total.astype(bf16)


def on_device(query_vectors, key_vectors, value_vectors, log_gate, doc_start, norm_gain, out_weight):
    bf16, f32 = jnp.bfloat16, jnp.float32
    block, _, size = key_vectors.shape
    row_width = query_vectors.shape[2]
    features = size * (size + 1) // 2
    slots = lax.axis_size("ctx")
    heads = lax.axis_size("heads")
    width = out_weight.shape[1] // heads
    span = min(CHUNK, slots) * block
    vmem = pl.BlockSpec(memory_space=pltpu.VMEM)
    mixed_out, prefix = pl.pallas_call(
        functools.partial(kernel, slots, heads),
        out_shape=(
            jax.ShapeDtypeStruct((block, width), bf16),
            jax.ShapeDtypeStruct((features, size), bf16),
        ),
        in_specs=[vmem] * 4
        + [pl.BlockSpec(memory_space=pltpu.SMEM), vmem, pl.BlockSpec(memory_space=pl.ANY)],
        out_specs=(vmem, vmem),
        scratch_shapes=[
            pltpu.VMEM((slots, 2 * block + EXTRA, size), bf16),
            pltpu.VMEM((1, slots * block), f32),
            pltpu.VMEM((heads, row_width, width), bf16),
            pltpu.VMEM((block, row_width), bf16),
            pltpu.VMEM((heads, block, width), bf16),
            pltpu.VMEM((heads - 1, block, width), bf16),
            pltpu.VMEM((size, span), bf16),
            pltpu.VMEM((size, span), f32),
            pltpu.VMEM((span, size), bf16),
            pltpu.VMEM((features, size), f32),
            pltpu.SemaphoreType.DMA((heads,)),
            pltpu.SemaphoreType.DMA((slots - 1,)),
            pltpu.SemaphoreType.DMA((slots,)),
            pltpu.SemaphoreType.DMA((heads - 1,)),
            pltpu.SemaphoreType.DMA((heads - 1,)),
        ],
        compiler_params=pltpu.CompilerParams(
            collective_id=0, has_side_effects=True, vmem_limit_bytes=56 * 2**20
        ),
    )(
        query_vectors[:, 0, :], key_vectors[:, 0, :], value_vectors[:, 0, :],
        log_gate, doc_start, norm_gain, out_weight,
    )
    return (mixed_out, prefix[None, None])


def solution(mesh):
    placed = (
        P("ctx", "heads", None),
        P("ctx", "heads", None),
        P("ctx", "heads", None),
        P("heads", "ctx"),
        P("ctx"),
        P("heads", None),
        P("heads", None),
    )
    return jax.shard_map(
        on_device,
        mesh=mesh,
        in_specs=placed,
        out_specs=(P("ctx", "heads"), P("heads", "ctx", None, None)),
        check_vma=False,
    )
```

time: 74.4 us -> 39.6 us (0.53)
  Pallas kernels: 10.4 us -> 33.8 us
  waiting for transfers between devices: 21.5 us -> 0 us
  blocking collectives: 16.6 us -> 0 us
  between operations: 14.7 us -> 1.29 us
  matrix products: 5.19 us -> 0 us
  other arithmetic: 3.83 us -> 0 us
  local copies, waits for them, and re-layouts: 1.79 us -> 4.33 us
    pallas_call x2 -> x1, Pallas kernels: 10.4 us -> 33.8 us  [on_device(): pl.pallas_call(functools.partial(kernel, slots, heads), out_shape=(jax.Sh...]
    reduce_scatter x1 -> x0, waiting for transfers between devices: 21.5 us -> none  [on_device(): lax.psum_scatter(partial, 'heads', scatter_dimension=1, tiled=True)]
    all_gather x1 -> x0, blocking collectives: 16.6 us -> none  [on_device(): gathered = lax.all_gather(sent, 'ctx', axis=0, tiled=False)]
    dot_general x1 -> x0, matrix products: 5.19 us -> none  [on_device(): jnp.dot(retained, out_weight, preferred_element_type=f32).astype(bf16)]
    unnamed x4 -> x2, local copies, waits for them, and re-layouts: 1.61 us -> 4.33 us
    concatenate x3 -> x0, other arithmetic: 1.58 us -> none  [the longest x1 0.79 us: on_device(): sent = jnp.concatenate([own, jnp.pad(extra, ((0, 14), (0, 0)))], axis=0)]
    reduce_sum x3 -> x0, other arithmetic: 1.09 us -> none  [the longest x1 0.76 us: on_device(): jnp.sum(jnp.where(token[:, None] >= token[None, :], gate, 0.0), axis=1)]
  transfers between devices with their start and end apart: 1 -> 0, of which waited for: 1 -> 0; matrix products, arithmetic and copies ran while one was open for 0% -> 0% of each run, Pallas kernels for 12% -> 0%
where the time goes in v1:
time: 39.6 us; the launch traced here: 39.4 us
  Pallas kernels  33.8 us (85%)
  local copies, waits for them, and re-layouts  4.33 us (11%)
  between operations  1.29 us (3%)
    pallas_call x1, Pallas kernels, on_device(): pl.pallas_call(functools.partial(kernel, slots, heads), out_shape=(jax.Sh...  33.8 us
    unnamed x2, local copies, waits for them, and re-layouts  4.33 us

profile of v1, /device:TPU:0, one launch (start us, length us, event | category | flops | bytes accessed | tf_op | source)
XLA Modules:
  0.0 39.4 jit_solution(10563427886613120339)
XLA Ops:
  1.3 33.8 %shard_map.86 = (bf16[128,1280]{1,0:T(8,128)(2,1)}, bf16[8256,128]{1,0:T(8,128)(2,1)}) custom-call(bf16[128,640]{1,0:T(8,128)(2,1)} %bitcast.5, bf16[128,128]{1,0:T(8,128)(2,1)} %bitcast.6, bf16[128,128]{1,0:T(8,128)(2,1)} %bitcast.7, f32[1,128]{1,0:T(1,128)} %gate_ref.1, s32[1]{0:T(128)S(6)} %copy.11.doc_ref, f32[1,640]{1,0:T(1,128)} %gain_ref.1, ...), custom_call_target="tpu_custom_call" | custom-call | tf_op jit(solution)/shard_map/pallas_call | solution.py:246
  35.1 1.7 %copy.12 = bf16[128,1280]{1,0:T(8,128)(2,1)} copy(bf16[128,1280]{1,0:T(8,128)(2,1)} %get-tuple-element.8) | data formatting | bytes 655360
  36.8 2.6 %copy.13 = bf16[1,1,8256,128]{3,2,1,0:T(8,128)(2,1)} copy(bf16[1,1,8256,128]{3,2,1,0:T(8,128)(2,1)} %bitcast.4) | data formatting | bytes 4227072

commit v2 on v1

--- a/solution.py
+++ b/solution.py
@@ -11,7 +11,7 @@
 ROOT_TWO = math.sqrt(2.0)
 NT = (((1,), (1,)), ((), ()))
 MESH = pl.DeviceIdType.MESH
-PER_STEP = 8
+PER_STEP = 16
 CHUNK = 8
 EXTRA = 16
 
@@ -58,10 +58,12 @@
     line = [lax.rem(outer + o, outers) * 2 + core for o in range(1, outers)]
     for peer in [twin] + line:
         pl.semaphore_signal(barrier, inc=1, device_id={"ctx": peer}, device_id_type=MESH)
-    for o in range(1, heads):
-        pl.semaphore_signal(
-            barrier, inc=1, device_id={"heads": lax.rem(head + o, heads)}, device_id_type=MESH
-        )
+    high_bit, low_bit = head // 2, head % 2
+    first_peer = high_bit * 2 + 1 - low_bit
+    second_peer = (1 - high_bit) * 2 + low_bit
+    across = (1 - high_bit) * 2 + 1 - low_bit
+    for peer in (first_peer, second_peer):
+        pl.semaphore_signal(barrier, inc=1, device_id={"heads": peer}, device_id_type=MESH)
 
     gate = gate_ref[...]
     high = gate.astype(bf16)
@@ -77,7 +79,7 @@
         axis=0,
     ).astype(bf16)
 
-    pl.semaphore_wait(barrier, outers + heads - 1)
+    pl.semaphore_wait(barrier, outers + 2)
 
     def move(slot, peer, index):
         return pltpu.make_async_remote_copy(
@@ -113,14 +115,32 @@
 
     summed = part(k_ref[...], v_ref[...], decay)
 
+    per = min(CHUNK, slots)
+    chunks = slots // per
+    span = per * block
+
+    def turn(slot, index):
+        lanes = pl.ds(pl.multiple_of(index * block, block), block)
+        turned = shared[slot, :block, :].astype(f32).T
+        keys_t[:, lanes] = turned.astype(bf16)
+        scaled[:, lanes] = turned
+        values[lanes, :] = shared[slot, block : 2 * block, :]
+
+    if chunks == 1:
+        turn(me, me)
+
     for o in range(1, outers):
         source = lax.rem(outer + outers - o, outers) * 2 + core
         move(source, twin, 0).wait_recv()
         sends.append(move(source, twin, outers - 1 + o))
         sends[-1].start()
+        if chunks == 1:
+            turn(source, source)
     for o in range(outers):
         source = lax.rem(outer + outers - o, outers) * 2 + 1 - core
         move(source, twin, 0).wait_recv()
+        if chunks == 1:
+            turn(source, source)
 
     tails = [shared[c, 2 * block :, :].astype(f32) for c in range(slots)]
     cumulative = running_sum(
@@ -141,7 +161,6 @@
         later = later + total * before
         alive = alive * jnp.where(broken, 1.0 - before, 1.0)
 
-    per = min(CHUNK, slots)
     for first in range(0, slots, per):
         keys = shared[first : first + per, :block, :].reshape(per * block, size)
         held = shared[first : first + per, block : 2 * block, :].reshape(per * block, size)
@@ -155,38 +174,59 @@
         lanes = slice(g * size, (g + 1) * size)
         retained[:, lanes] = (normed[g * block : (g + 1) * block] * gain_ref[:, lanes]).astype(bf16)
 
+    half = width // 2
+
+    def project(target, index):
+        product = jnp.dot(retained[...], projection[target], preferred_element_type=f32).astype(bf16)
+        outgoing[2 * index] = product[:, :half]
+        outgoing[2 * index + 1] = product[:, half:]
+
+    def part_copy(index, held, peer):
+        return pltpu.make_async_remote_copy(
+            src_ref=outgoing.at[held],
+            dst_ref=incoming.at[index],
+            send_sem=part_send.at[index],
+            recv_sem=part_recv.at[index],
+            device_id={"heads": peer},
+            device_id_type=MESH,
+        )
+
+    copies = [
+        part_copy(0, 6, first_peer),
+        part_copy(1, 7, second_peer),
+        part_copy(2, 2, first_peer),
+        part_copy(3, 5, second_peer),
+        part_copy(4, 3, first_peer),
+        part_copy(5, 4, second_peer),
+    ]
     for load in loads:
         load.wait()
-    parts = []
-    for o in list(range(1, heads)) + [0]:
-        target = lax.rem(head + o, heads)
-        outgoing[o] = jnp.dot(
-            retained[...], projection[target], preferred_element_type=f32
-        ).astype(bf16)
-        if o:
-            parts.append(
-                pltpu.make_async_remote_copy(
-                    src_ref=outgoing.at[o],
-                    dst_ref=incoming.at[o - 1],
-                    send_sem=part_send.at[o - 1],
-                    recv_sem=part_recv.at[o - 1],
-                    device_id={"heads": target},
-                    device_id_type=MESH,
-                )
-            )
-            parts[-1].start()
-
-    chunks = slots // per
-    span = per * block
+    project(across, 3)
+    copies[0].start()
+    copies[1].start()
+    project(first_peer, 1)
+    copies[2].start()
+    project(second_peer, 2)
+    copies[3].start()
+    project(head, 0)
+
+    def pass_on():
+        copies[1].wait_recv()
+        outgoing[3] = (outgoing[3].astype(f32) + incoming[1].astype(f32)).astype(bf16)
+        copies[4].start()
+        copies[0].wait_recv()
+        outgoing[4] = (outgoing[4].astype(f32) + incoming[0].astype(f32)).astype(bf16)
+        copies[5].start()
 
     def chunk(index):
-        for c in range(per):
-            lanes = slice(c * block, (c + 1) * block)
-            turned = shared[index * per + c, :block, :].astype(f32).T
-            keys_t[:, lanes] = turned.astype(bf16)
-            weight = token_weight[:, pl.ds(pl.multiple_of((index * per + c) * block, block), block)]
-            scaled[:, lanes] = turned * weight
-            values[lanes, :] = shared[index * per + c, block : 2 * block, :]
+        if chunks == 1:
+            scaled[...] = scaled[...] * token_weight[...]
+        else:
+            for c in range(per):
+                lanes = slice(c * block, (c + 1) * block)
+                turn(index * per + c, c)
+                weight = token_weight[:, pl.ds(pl.multiple_of((index * per + c) * block, block), block)]
+                scaled[:, lanes] = scaled[:, lanes] * weight
         for a in range(size - 16, -1, -16):
             rows = size - a
 
@@ -215,22 +255,38 @@
                 return carry
 
             lax.fori_loop(0, 16 // PER_STEP, step, 0)
+            if chunks == 1 and a == size // 2:
+                pass_on()
 
     if chunks == 1:
         chunk(0)
     else:
+        pass_on()
         acc[...] = jnp.zeros_like(acc)
         lax.fori_loop(0, chunks, lambda index, carry: (chunk(index), carry)[1], 0)
     prefix_ref[...] = acc[...].astype(bf16)
 
     for send in sends:
         send.wait_send()
-    for send in parts:
-        send.wait()
-    total = outgoing[0].astype(f32)
-    for o in range(1, heads):
-        total = total + incoming[o - 1].astype(f32)
-    mixed_ref[...] = total.astype(bf16)
+    for copy in copies:
+        copy.wait_send()
+    for copy in copies[2:]:
+        copy.wait_recv()
+    for side, (one, two) in enumerate(((2, 5), (3, 4))):
+        total = outgoing[side].astype(f32) + incoming[one].astype(f32) + incoming[two].astype(f32)
+        mixed_ref[:, side * half : (side + 1) * half] = total.astype(bf16)
+
+
+def place_kernel(cuts, mixed_in, prefix_in, mixed_ref, prefix_ref, sems):
+    rows = prefix_ref.shape[0] // cuts
+    copies = [pltpu.make_async_copy(mixed_in, mixed_ref, sems.at[cuts])]
+    for c in range(cuts):
+        part = pl.ds(c * rows, rows)
+        copies.append(pltpu.make_async_copy(prefix_in.at[part], prefix_ref.at[part], sems.at[c]))
+    for copy in copies:
+        copy.start()
+    for copy in copies:
+        copy.wait()
 
 
 def on_device(query_vectors, key_vectors, value_vectors, log_gate, doc_start, norm_gain, out_weight):
@@ -243,22 +299,23 @@
     width = out_weight.shape[1] // heads
     span = min(CHUNK, slots) * block
     vmem = pl.BlockSpec(memory_space=pltpu.VMEM)
-    mixed_out, prefix = pl.pallas_call(
+    shapes = (
+        jax.ShapeDtypeStruct((block, width), bf16),
+        jax.ShapeDtypeStruct((features, size), bf16),
+    )
+    results = pl.pallas_call(
         functools.partial(kernel, slots, heads),
-        out_shape=(
-            jax.ShapeDtypeStruct((block, width), bf16),
-            jax.ShapeDtypeStruct((features, size), bf16),
-        ),
+        out_shape=shapes,
         in_specs=[vmem] * 4
-        + [pl.BlockSpec(memory_space=pltpu.SMEM), vmem, pl.BlockSpec(memory_space=pl.ANY)],
+        + [pl.BlockSpec(memory_space=pltpu.SMEM), vmem, pl.BlockSpec(memory_space=pltpu.HBM)],
         out_specs=(vmem, vmem),
         scratch_shapes=[
             pltpu.VMEM((slots, 2 * block + EXTRA, size), bf16),
             pltpu.VMEM((1, slots * block), f32),
             pltpu.VMEM((heads, row_width, width), bf16),
             pltpu.VMEM((block, row_width), bf16),
-            pltpu.VMEM((heads, block, width), bf16),
-            pltpu.VMEM((heads - 1, block, width), bf16),
+            pltpu.VMEM((2 * heads, block, width // 2), bf16),
+            pltpu.VMEM((6, block, width // 2), bf16),
             pltpu.VMEM((size, span), bf16),
             pltpu.VMEM((size, span), f32),
             pltpu.VMEM((span, size), bf16),
@@ -266,16 +323,26 @@
             pltpu.SemaphoreType.DMA((heads,)),
             pltpu.SemaphoreType.DMA((slots - 1,)),
             pltpu.SemaphoreType.DMA((slots,)),
-            pltpu.SemaphoreType.DMA((heads - 1,)),
-            pltpu.SemaphoreType.DMA((heads - 1,)),
+            pltpu.SemaphoreType.DMA((6,)),
+            pltpu.SemaphoreType.DMA((6,)),
         ],
         compiler_params=pltpu.CompilerParams(
-            collective_id=0, has_side_effects=True, vmem_limit_bytes=56 * 2**20
+            collective_id=0, has_side_effects=True, vmem_limit_bytes=50 * 2**20
         ),
     )(
         query_vectors[:, 0, :], key_vectors[:, 0, :], value_vectors[:, 0, :],
         log_gate, doc_start, norm_gain, out_weight,
     )
+    anywhere = pl.BlockSpec(memory_space=pl.ANY)
+    cuts = 4 if features % 64 == 0 else 1
+    mixed_out, prefix = pl.pallas_call(
+        functools.partial(place_kernel, cuts),
+        out_shape=shapes,
+        in_specs=[anywhere] * 2,
+        out_specs=(anywhere, anywhere),
+        scratch_shapes=[pltpu.SemaphoreType.DMA((cuts + 1,))],
+        compiler_params=pltpu.CompilerParams(vmem_limit_bytes=2**20),
+    )(*results)
     return (mixed_out, prefix[None, None])
 
 

time: 39.6 us -> 35 us (0.88)
  Pallas kernels: 33.8 us -> 29.6 us
  local copies, waits for them, and re-layouts: 4.33 us -> 3.76 us
    pallas_call x1 -> x2, Pallas kernels: 33.8 us -> 29.6 us  [the longest x1 28.1 us: on_device(): pl.pallas_call(functools.partial(kernel, slots, heads), out_shape=shapes,...]
    unnamed x2 -> x10, local copies, waits for them, and re-layouts: 4.33 us -> 3.76 us
where the time goes in v2:
time: 35 us; the launch traced here: 34.7 us
  Pallas kernels  29.6 us (85%)
  local copies, waits for them, and re-layouts  3.76 us (11%)
  between operations  1.3 us (4%)
    pallas_call x1, Pallas kernels, on_device(): pl.pallas_call(functools.partial(kernel, slots, heads), out_shape=shapes,...  28.1 us
    unnamed x10, local copies, waits for them, and re-layouts  3.76 us
    pallas_call x1, Pallas kernels, on_device(): pl.pallas_call(functools.partial(place_kernel, cuts), out_shape=shapes, i...  1.47 us

profile of v2, /device:TPU:0, one launch (start us, length us, event | category | flops | bytes accessed | tf_op | source)
XLA Modules:
  0.0 34.7 jit_solution(8453466788898239565)
XLA Ops:
  1.3 0.0 copy-start
  1.3 0.9 %copy-done = bf16[128,1,640]{2,0,1:T(8,128)(2,1)S(1)} copy-done((bf16[128,1,640]{2,0,1:T(8,128)(2,1)S(1)}, bf16[128,1,640]{2,0,1:T(8,128)(2,1)}, u32[]{:S(2)}) %copy-start) | copy-done | bytes 163864
  2.2 0.0 copy-start.1
  2.2 0.8 %copy-done.1 = bf16[128,1,128]{2,0,1:T(8,128)(2,1)S(1)} copy-done((bf16[128,1,128]{2,0,1:T(8,128)(2,1)S(1)}, bf16[128,1,128]{2,0,1:T(8,128)(2,1)}, u32[]{:S(2)}) %copy-start.1) | copy-done | bytes 32792
  3.0 0.0 copy-start.2
  3.0 0.8 %copy-done.2 = bf16[128,1,128]{2,0,1:T(8,128)(2,1)S(1)} copy-done((bf16[128,1,128]{2,0,1:T(8,128)(2,1)S(1)}, bf16[128,1,128]{2,0,1:T(8,128)(2,1)}, u32[]{:S(2)}) %copy-start.2) | copy-done | bytes 32792
  3.7 0.0 copy-start.3
  3.7 0.7 %copy-done.3 = f32[1,640]{1,0:T(1,128)S(1)} copy-done((f32[1,640]{1,0:T(1,128)S(1)}, f32[1,640]{1,0:T(1,128)}, u32[]{:S(2)}) %copy-start.3) | copy-done | bytes 2584
  4.4 0.0 copy-start.4
  4.4 0.7 %copy-done.4 = f32[1,128]{1,0:T(1,128)S(1)} copy-done((f32[1,128]{1,0:T(1,128)S(1)}, f32[1,128]{1,0:T(1,128)}, u32[]{:S(2)}) %copy-start.4) | copy-done | bytes 536
  5.1 28.1 %shard_map.86 = (bf16[128,1280]{1,0:T(8,128)(2,1)S(1)}, bf16[8256,128]{1,0:T(8,128)(2,1)S(1)}) custom-call(bf16[128,640]{1,0:T(8,128)(2,1)S(1)} %bitcast.4, bf16[128,128]{1,0:T(8,128)(2,1)S(1)} %bitcast.5, bf16[128,128]{1,0:T(8,128)(2,1)S(1)} %bitcast.6, f32[1,128]{1,0:T(1,128)S(1)} %copy-done.4, s32[1]{0:T(128)S(6)} %copy.9.doc_ref, ...), custom_call_target="tpu_custom_call" | custom-call | tf_op jit(solution)/shard_map/pallas_call | solution.py:306
  33.2 1.5 %shard_map.87 = (bf16[128,1280]{1,0:T(8,128)(2,1)}, bf16[8256,128]{1,0:T(8,128)(2,1)}) custom-call(bf16[128,1280]{1,0:T(8,128)(2,1)S(1)} %get-tuple-element.6.mixed_in, bf16[8256,128]{1,0:T(8,128)(2,1)S(1)} %get-tuple-element.7.prefix_in), custom_call_target="tpu_custom_call" | custom-call | tf_op jit(solution)/shard_map/pallas_call | solution.py:338
Async XLA Ops:
  1.3 0.9 %copy-start = (bf16[128,1,640]{2,0,1:T(8,128)(2,1)S(1)}, bf16[128,1,640]{2,0,1:T(8,128)(2,1)}, u32[]{:S(2)}) copy-start(bf16[128,1,640]{2,0,1:T(8,128)(2,1)} %param.7) | copy-start | bytes 491524
  2.2 0.8 %copy-start.1 = (bf16[128,1,128]{2,0,1:T(8,128)(2,1)S(1)}, bf16[128,1,128]{2,0,1:T(8,128)(2,1)}, u32[]{:S(2)}) copy-start(bf16[128,1,128]{2,0,1:T(8,128)(2,1)} %param.8) | copy-start | bytes 98308
  3.0 0.8 %copy-start.2 = (bf16[128,1,128]{2,0,1:T(8,128)(2,1)S(1)}, bf16[128,1,128]{2,0,1:T(8,128)(2,1)}, u32[]{:S(2)}) copy-start(bf16[128,1,128]{2,0,1:T(8,128)(2,1)} %param.9) | copy-start | bytes 98308
  3.7 0.7 %copy-start.3 = (f32[1,640]{1,0:T(1,128)S(1)}, f32[1,640]{1,0:T(1,128)}, u32[]{:S(2)}) copy-start(f32[1,640]{1,0:T(1,128)} %gain_ref.1) | copy-start | bytes 7684
  4.4 0.7 %copy-start.4 = (f32[1,128]{1,0:T(1,128)S(1)}, f32[1,128]{1,0:T(1,128)}, u32[]{:S(2)}) copy-start(f32[1,128]{1,0:T(1,128)} %gate_ref.1) | copy-start | bytes 1540

commit v3 on v2

--- a/solution.py
+++ b/solution.py
@@ -32,8 +32,8 @@
 def kernel(
     slots, heads, q_ref, k_ref, v_ref, gate_ref, doc_ref, gain_ref, weight_hbm,
     mixed_ref, prefix_ref,
-    shared, token_weight, projection, retained, outgoing, incoming, keys_t, scaled, values, acc,
-    load_sem, gather_send, gather_recv, part_send, part_recv,
+    shared, token_weight, projection, retained, outgoing, incoming, keys_t, scaled, values, acc, staged,
+    store_sem, load_sem, gather_send, gather_recv, part_send, part_recv,
 ):
     bf16, f32 = jnp.bfloat16, jnp.float32
     block, size = k_ref.shape
@@ -217,6 +217,18 @@
         copies[0].wait_recv()
         outgoing[4] = (outgoing[4].astype(f32) + incoming[0].astype(f32)).astype(bf16)
         copies[5].start()
+
+    stores = []
+
+    def emit(a):
+        low_row = -(-offset(a, size) // 16) * 16
+        high_row = prefix_ref.shape[0] if a == size - 16 else -(-offset(a + 16, size) // 16) * 16
+        rows = pl.ds(low_row, high_row - low_row)
+        staged[rows, :] = acc[rows, :].astype(bf16)
+        stores.append(
+            pltpu.make_async_copy(staged.at[rows], prefix_ref.at[rows], store_sem.at[a // 16])
+        )
+        stores[-1].start()
 
     def chunk(index):
         if chunks == 1:
@@ -255,6 +267,8 @@
                 return carry
 
             lax.fori_loop(0, 16 // PER_STEP, step, 0)
+            if chunks == 1:
+                emit(a)
             if chunks == 1 and a == size // 2:
                 pass_on()
 
@@ -264,10 +278,13 @@
         pass_on()
         acc[...] = jnp.zeros_like(acc)
         lax.fori_loop(0, chunks, lambda index, carry: (chunk(index), carry)[1], 0)
-    prefix_ref[...] = acc[...].astype(bf16)
+        for a in range(size - 16, -1, -16):
+            emit(a)
 
     for send in sends:
         send.wait_send()
+    for copy in stores:
+        copy.wait()
     for copy in copies:
         copy.wait_send()
     for copy in copies[2:]:
@@ -308,7 +325,7 @@
         out_shape=shapes,
         in_specs=[vmem] * 4
         + [pl.BlockSpec(memory_space=pltpu.SMEM), vmem, pl.BlockSpec(memory_space=pltpu.HBM)],
-        out_specs=(vmem, vmem),
+        out_specs=(vmem, pl.BlockSpec(memory_space=pl.ANY)),
         scratch_shapes=[
             pltpu.VMEM((slots, 2 * block + EXTRA, size), bf16),
             pltpu.VMEM((1, slots * block), f32),
@@ -320,6 +337,8 @@
             pltpu.VMEM((size, span), f32),
             pltpu.VMEM((span, size), bf16),
             pltpu.VMEM((features, size), f32),
+            pltpu.VMEM((features, size), bf16),
+            pltpu.SemaphoreType.DMA((size // 16,)),
             pltpu.SemaphoreType.DMA((heads,)),
             pltpu.SemaphoreType.DMA((slots - 1,)),
             pltpu.SemaphoreType.DMA((slots,)),
@@ -327,7 +346,7 @@
             pltpu.SemaphoreType.DMA((6,)),
         ],
         compiler_params=pltpu.CompilerParams(
-            collective_id=0, has_side_effects=True, vmem_limit_bytes=50 * 2**20
+            collective_id=0, has_side_effects=True, vmem_limit_bytes=54 * 2**20
         ),
     )(
         query_vectors[:, 0, :], key_vectors[:, 0, :], value_vectors[:, 0, :],
@@ -341,7 +360,7 @@
         in_specs=[anywhere] * 2,
         out_specs=(anywhere, anywhere),
         scratch_shapes=[pltpu.SemaphoreType.DMA((cuts + 1,))],
-        compiler_params=pltpu.CompilerParams(vmem_limit_bytes=2**20),
+        compiler_params=pltpu.CompilerParams(vmem_limit_bytes=54 * 2**20),
     )(*results)
     return (mixed_out, prefix[None, None])
 

time: 35 us -> 106 us (3.03)
  Pallas kernels: 29.6 us -> 105 us
  local copies, waits for them, and re-layouts: 3.76 us -> 0 us
    pallas_call x1, Pallas kernels: 1.47 us -> 75.1 us  [on_device(): pl.pallas_call(functools.partial(place_kernel, cuts), out_shape=shapes, i...]
    unnamed x10 -> x0, local copies, waits for them, and re-layouts: 3.76 us -> none
    pallas_call x1, Pallas kernels: 28.1 us -> 29.9 us  [on_device(): pl.pallas_call(functools.partial(kernel, slots, heads), out_shape=shapes,...]
where the time goes in v3:
time: 106 us
  Pallas kernels  105 us (99%)
  between operations  1.29 us (1%)
    pallas_call x1, Pallas kernels, on_device(): pl.pallas_call(functools.partial(place_kernel, cuts), out_shape=shapes, i...  75.1 us
    pallas_call x1, Pallas kernels, on_device(): pl.pallas_call(functools.partial(kernel, slots, heads), out_shape=shapes,...  29.9 us

profile of v3, /device:TPU:0, one launch (start us, length us, event | category | flops | bytes accessed | tf_op | source)
XLA Modules:
  0.0 106.3 jit_solution(11097015827991091674)
XLA Ops:
  1.3 29.9 %shard_map.86 = (bf16[128,1280]{1,0:T(8,128)(2,1)}, bf16[8256,128]{1,0:T(8,128)(2,1)}) custom-call(bf16[128,640]{1,0:T(8,128)(2,1)} %bitcast.4, bf16[128,128]{1,0:T(8,128)(2,1)} %bitcast.5, bf16[128,128]{1,0:T(8,128)(2,1)} %bitcast.6, f32[1,128]{1,0:T(1,128)} %gate_ref.1, s32[1]{0:T(128)S(6)} %copy.9.doc_ref, f32[1,640]{1,0:T(1,128)} %gain_ref.1, ...), custom_call_target="tpu_custom_call" | custom-call | tf_op jit(solution)/shard_map/pallas_call | solution.py:323
  31.2 75.1 %shard_map.87 = (bf16[128,1280]{1,0:T(8,128)(2,1)}, bf16[8256,128]{1,0:T(8,128)(2,1)}) custom-call(bf16[128,1280]{1,0:T(8,128)(2,1)} %get-tuple-element.6.mixed_in, bf16[8256,128]{1,0:T(8,128)(2,1)} %get-tuple-element.7.prefix_in), custom_call_target="tpu_custom_call" | custom-call | tf_op jit(solution)/shard_map/pallas_call | solution.py:357

commit v4 on v3

--- a/solution.py
+++ b/solution.py
@@ -294,15 +294,26 @@
         mixed_ref[:, side * half : (side + 1) * half] = total.astype(bf16)
 
 
-def place_kernel(cuts, mixed_in, prefix_in, mixed_ref, prefix_ref, sems):
+def place_kernel(cuts, mixed_in, prefix_in, mixed_ref, prefix_ref, mixed_held, prefix_held, sems):
     rows = prefix_ref.shape[0] // cuts
-    copies = [pltpu.make_async_copy(mixed_in, mixed_ref, sems.at[cuts])]
+    inward = []
+    outward = []
     for c in range(cuts):
         part = pl.ds(c * rows, rows)
-        copies.append(pltpu.make_async_copy(prefix_in.at[part], prefix_ref.at[part], sems.at[c]))
-    for copy in copies:
+        inward.append(
+            pltpu.make_async_copy(prefix_in.at[part], prefix_held.at[part], sems.at[0, c])
+        )
+        outward.append(
+            pltpu.make_async_copy(prefix_held.at[part], prefix_ref.at[part], sems.at[1, c])
+        )
+    inward.append(pltpu.make_async_copy(mixed_in, mixed_held, sems.at[0, cuts]))
+    outward.append(pltpu.make_async_copy(mixed_held, mixed_ref, sems.at[1, cuts]))
+    for copy in inward:
         copy.start()
-    for copy in copies:
+    for get, put in zip(inward, outward):
+        get.wait()
+        put.start()
+    for copy in outward:
         copy.wait()
 
 
@@ -359,7 +370,11 @@
         out_shape=shapes,
         in_specs=[anywhere] * 2,
         out_specs=(anywhere, anywhere),
-        scratch_shapes=[pltpu.SemaphoreType.DMA((cuts + 1,))],
+        scratch_shapes=[
+            pltpu.VMEM((block, width), bf16),
+            pltpu.VMEM((features, size), bf16),
+            pltpu.SemaphoreType.DMA((2, cuts + 1)),
+        ],
         compiler_params=pltpu.CompilerParams(vmem_limit_bytes=54 * 2**20),
     )(*results)
     return (mixed_out, prefix[None, None])

time: 106 us -> 33.9 us (0.32)
  Pallas kernels: 105 us -> 32.5 us
    pallas_call x1, Pallas kernels: 75.1 us -> 2.55 us  [on_device(): pl.pallas_call(functools.partial(place_kernel, cuts), out_shape=shapes, i...]
where the time goes in v4:
time: 33.9 us; the launch traced here: 33.7 us
  Pallas kernels  32.5 us (96%)
  between operations  1.29 us (4%)
    pallas_call x1, Pallas kernels, on_device(): pl.pallas_call(functools.partial(kernel, slots, heads), out_shape=shapes,...  29.9 us
    pallas_call x1, Pallas kernels, on_device(): pl.pallas_call(functools.partial(place_kernel, cuts), out_shape=shapes, i...  2.55 us

profile of v4, /device:TPU:0, one launch (start us, length us, event | category | flops | bytes accessed | tf_op | source)
XLA Modules:
  0.0 33.7 jit_solution(2372992619375051267)
XLA Ops:
  1.3 29.9 %shard_map.86 = (bf16[128,1280]{1,0:T(8,128)(2,1)}, bf16[8256,128]{1,0:T(8,128)(2,1)}) custom-call(bf16[128,640]{1,0:T(8,128)(2,1)} %bitcast.4, bf16[128,128]{1,0:T(8,128)(2,1)} %bitcast.5, bf16[128,128]{1,0:T(8,128)(2,1)} %bitcast.6, f32[1,128]{1,0:T(1,128)} %gate_ref.1, s32[1]{0:T(128)S(6)} %copy.9.doc_ref, f32[1,640]{1,0:T(1,128)} %gain_ref.1, ...), custom_call_target="tpu_custom_call" | custom-call | tf_op jit(solution)/shard_map/pallas_call | solution.py:334
  31.2 2.6 %shard_map.87 = (bf16[128,1280]{1,0:T(8,128)(2,1)}, bf16[8256,128]{1,0:T(8,128)(2,1)}) custom-call(bf16[128,1280]{1,0:T(8,128)(2,1)} %get-tuple-element.6.mixed_in, bf16[8256,128]{1,0:T(8,128)(2,1)} %get-tuple-element.7.prefix_in), custom_call_target="tpu_custom_call" | custom-call | tf_op jit(solution)/shard_map/pallas_call | solution.py:368
